TPU v7x, 256 devices: a whole 4x4x8 slice. The times are simulated.
256 devices in a mesh: dp: 16 (over z, core), expert: 4 (over y), blk: 4 (over x).
Axes of the slice: x: 4, y: 4, z: 8, core: 2. Of those that a mesh axis runs over, the one named last changes fastest.
Arguments:
- tokens: bfloat16 [2048, 6144], P('dp', 'blk'), may hold values from -6 to 6
- expert_ids: int32 [2048, 2], P('dp'), may hold values from 0 to 7, all different within a row; in each aligned block of 128 rows (0 to 127, 128 to 255, ...) at most 48 rows name the same one
- route_weights: float32 [2048, 2], P('dp'), may hold values from 0.1 to 1
- gate_weight: bfloat16 [8, 6144, 8192], P('expert', 'blk', 'dp'), may hold values from -0.078125 to 0.078125
- up_weight: bfloat16 [8, 6144, 8192], P('expert', 'blk', 'dp'), may hold values from -0.078125 to 0.078125
- down_weight: bfloat16 [8, 8192, 6144], P('expert', 'dp', 'blk'), may hold values from -0.0625 to 0.0625
Outputs:
- mixed: bfloat16 [2048, 6144], P('dp', 'blk')
Inputs may be any that keep to these rules, and one draw needn't show every extreme that they name: `expert_ids`: each row names 2 different experts. Among the 128 rows of one data shard no expert is named more than 48 times, and in every draw some expert is named exactly 48 times in some shard.
All inputs are finite; a program needn't handle non-finite values.
Results may differ from a plain program's by a relative error of at most 0.0051.
Values may be sent and summed in bfloat16 or wider, within the bound.
A program may use at most 64 MiB of HBM per device.

v0:
```python
import jax
import jax.numpy as jnp
from jax import lax
from jax.sharding import PartitionSpec as P

EXPERTS = 8
CAP = 48


def local(tokens, expert_ids, route_weights, gate_weight, up_weight, down_weight):
    local_count = gate_weight.shape[0]
    token_count = tokens.shape[0]
    top_count = expert_ids.shape[1]
    group_index = lax.axis_index("expert")
    flat_ids = expert_ids.reshape(-1)
    one_hot = (flat_ids[:, None] == jnp.arange(EXPERTS, dtype=jnp.int32)[None, :]).astype(jnp.int32)
    before = jnp.cumsum(one_hot, axis=0) - one_hot
    position = jnp.sum(before * one_hot, axis=1)
    local_ids = flat_ids - group_index * local_count
    is_mine = local_ids[:, None] == jnp.arange(local_count, dtype=jnp.int32)[None, :]
    in_slot = position[:, None] == jnp.arange(CAP, dtype=jnp.int32)[None, :]
    slot_hit = (is_mine[:, :, None] & in_slot[:, None, :]).reshape(
        token_count, top_count, local_count, CAP
    )
    dispatch = jnp.any(slot_hit, axis=1).astype(jnp.bfloat16)
    combine = jnp.sum(slot_hit.astype(jnp.float32) * route_weights[:, :, None, None], axis=1)
    picked = jnp.einsum("tec,tf->ecf", dispatch, tokens, preferred_element_type=jnp.float32).astype(
        jnp.bfloat16
    )
    shard_rows = lax.all_gather(picked, "dp", axis=1, tiled=True)
    gate_part = jnp.einsum(
        "enf,efh->enh", shard_rows, gate_weight, preferred_element_type=jnp.float32
    )
    up_part = jnp.einsum("enf,efh->enh", shard_rows, up_weight, preferred_element_type=jnp.float32)
    partial_value = jnp.stack([gate_part, up_part])
    summed = lax.psum(partial_value, "blk")
    hidden = (jax.nn.silu(summed[0]) * summed[1]).astype(jnp.bfloat16)
    expert_out = lax.psum_scatter(
        jnp.einsum("enh,ehd->ned", hidden, down_weight, preferred_element_type=jnp.float32),
        "dp",
        scatter_dimension=0,
        tiled=True,
    )
    mixed_part = jnp.einsum("tec,ced->td", combine, expert_out, precision=lax.Precision.HIGHEST)
    mixed = lax.psum(mixed_part, "expert")
    return mixed.astype(jnp.bfloat16)


def solution(mesh):
    placed = (
        P("dp", "blk"),
        P("dp", None),
        P("dp", None),
        P("expert", "blk", "dp"),
        P("expert", "blk", "dp"),
        P("expert", "dp", "blk"),
    )
    return jax.shard_map(
        local, mesh=mesh, in_specs=placed, out_specs=P("dp", "blk"), check_vma=False
    )
```

profile of v0, /device:TPU:2, one launch (start us, length us, event | category | flops | bytes accessed | tf_op | source)
XLA Modules:
  0.0 316.2 jit_solution(18314517861227424447)
XLA Ops:
  6.5 0.9 copy.13
  7.5 0.1 eq.65
  7.6 0.1 reshape.70
  7.8 0.6 reduce-window.6
  8.4 0.2 slice_reduce_fusion
  8.6 0.1 fusion.7
  8.7 0.1 eq.69
  8.9 0.1 copy.15
  9.0 0.7 broadcast_subtract_fusion
  9.7 1.9 convolution_convert_fusion
  11.7 0.0 all-reduce.3.cloned.1.call-start
  11.7 45.8 %all-gather.2.cloned.1.call-done = bf16[2,768,1536]{2,1,0:T(8,128)(2,1)} async-done(((bf16[2,48,1536]{2,1,0:T(8,128)(2,1)}), bf16[2,768,1536]{2,1,0:T(8,128)(2,1)}) %all-gather.2.cloned.1.call-update) | async-done | bytes 4718608 | tf_op jit(solution)/shard_map/all_gather | solution.py:30
  57.5 5.5 %convolution_bitcast_fusion.2 = f32[1,2,768,512]{3,2,1,0:T(8,128)S(1)} fusion(bf16[2,768,1536]{2,1,0:T(8,128)(2,1)} %all-gather.2.cloned.1.call-done, bf16[2,1536,512]{2,1,0:T(8,128)(2,1)} %param.10), kind=kOutput, calls=%fused_computation.8 | convolution fusion | flops 2415919104 | bytes 11010048 | tf_op jit(solution)/shard_map/enf,efh->enh/dot_general | solution.py:34
  63.0 0.1 copy-done.3
  63.1 2.6 convolution_bitcast_fusion.3
  65.7 3.4 %pad_maximum_fusion = f32[2,2,768,512]{3,2,1,0:T(8,128)} fusion(f32[1,2,768,512]{3,2,1,0:T(8,128)S(1)} %convolution_bitcast_fusion.2, f32[1,2,768,512]{3,2,1,0:T(8,128)S(1)} %convolution_bitcast_fusion.3), kind=kLoop, calls=%fused_computation | loop fusion | flops 1572864 | bytes 12582912 | tf_op jit(solution)/shard_map/stack | solution.py:35
  69.1 0.0 all-reduce.3.cloned.1.call-update
  69.1 0.0 reduce-scatter.2.cloned.1.call-start
  69.1 129.7 %all-reduce.3.cloned.1.call-done = f32[2,2,768,512]{3,2,1,0:T(8,128)} async-done(((f32[2,2,768,512]{3,2,1,0:T(8,128)}), f32[2,2,768,512]{3,2,1,0:T(8,128)}) %all-reduce.3.cloned.1.call-update) | async-done | bytes 6291472 | tf_op jit(solution)/shard_map/psum | solution.py:36
  198.9 8.0 %convolution_bitcast_fusion = f32[768,2,1536]{2,0,1:T(8,128)} fusion(bf16[2,512,1536]{2,1,0:T(8,128)(2,1)S(1)} %copy-done, f32[2,2,768,512]{3,2,1,0:T(8,128)} %all-reduce.3.cloned.1.call-done), kind=kOutput, calls=%fused_computation.1 | convolution fusion | flops 2420637696 | bytes 18874368 | tf_op jit(solution)/shard_map/enh,ehd->ned/dot_general | solution.py:39
  206.9 0.7 copy-done.1
  207.6 73.1 %reduce-scatter.2.cloned.1.call-done = f32[48,2,1536]{2,0,1:T(8,128)} async-done(((f32[768,2,1536]{2,0,1:T(8,128)}), f32[48,2,1536]{2,0,1:T(8,128)}) %reduce-scatter.2.cloned.1.call-update) | async-done | bytes 589840 | tf_op jit(solution)/shard_map/reduce_scatter | solution.py:38
  280.7 2.8 convolution_bitcast_fusion.1
  283.5 26.3 %all-reduce.4 = bf16[128,1536]{1,0:T(8,128)(2,1)} all-reduce(f32[128,1536]{1,0:T(8,128)} %convolution_bitcast_fusion.1), channel_id=1, replica_groups=mesh['dp'=16,'expert'=4,'blk'=4] {'expert'}, use_global_device_ids=true, to_apply=%region_7.8 | all-reduce | flops 196608 | bytes 1179648 | tf_op jit(solution)/shard_map/psum | solution.py:45
  (16 shorter events, 0.2 us)
Async XLA Ops:
  6.5 192.3 %copy-start = (bf16[2,512,1536]{2,1,0:T(8,128)(2,1)S(1)}, bf16[2,512,1536]{2,1,0:T(8,128)(2,1)}, u32[]{:S(2)}) copy-start(bf16[2,512,1536]{2,1,0:T(8,128)(2,1)} %param.11) | copy-start | bytes 9437188
  6.5 50.9 %all-gather.2.cloned.1.call-start = ((), (), s32[]{:S(2)}) async-start(), calls=%async_computation.1 | async-start | bytes 5013504 | tf_op jit(solution)/shard_map/all_gather | solution.py:30
  11.7 187.2 %all-reduce.3.cloned.1.call-start = ((), (), s32[]{:S(2)}) async-start(), calls=%async_computation.2 | async-start | bytes 12582912 | tf_op jit(solution)/shard_map/psum | solution.py:36
  57.5 5.6 %copy-start.2 = (bf16[2,768,1536]{2,1,0:T(8,128)(2,1)S(1)}, bf16[2,768,1536]{2,1,0:T(8,128)(2,1)}, u32[]{:S(2)}) copy-start(bf16[2,768,1536]{2,1,0:T(8,128)(2,1)} %all-gather.2.cloned.1.call-done) | copy-start | bytes 14155780
  57.5 5.6 %copy-start.3 = (bf16[2,1536,512]{2,1,0:T(8,128)(2,1)S(1)}, bf16[2,1536,512]{2,1,0:T(8,128)(2,1)}, u32[]{:S(2)}) copy-start(bf16[2,1536,512]{2,1,0:T(8,128)(2,1)} %param.9) | copy-start | bytes 9437188
  69.1 211.6 %reduce-scatter.2.cloned.1.call-start = ((), (), s32[]{:S(2)}) async-start(), calls=%async_computation.3 | async-start | bytes 10027008 | tf_op jit(solution)/shard_map/reduce_scatter | solution.py:38
  206.9 0.7 copy-start.1
Sparse Core Ops, SparseCore 0:
  11.8 45.6 all-gather.1
  69.2 129.6 all-reduce.2
  207.0 73.5 reduce-scatter.1
where the time goes:
time: 316 us
  waiting for transfers between devices  249 us (79%)
  blocking collectives  26.3 us (8%)
  matrix products  20.9 us (7%)
  between operations  13.2 us (4%)
  other arithmetic  4.85 us (2%)
    psum x1, waiting for transfers between devices, local(): summed = lax.psum(partial_value, 'blk')  130 us
    reduce_scatter x1, waiting for transfers between devices, local(): lax.psum_scatter(jnp.einsum('enh,ehd->ned', hidden, down_weight, preferre...  73.1 us
    all_gather x1, waiting for transfers between devices, local(): shard_rows = lax.all_gather(picked, 'dp', axis=1, tiled=True)  45.8 us
    psum x1, blocking collectives, local(): mixed = lax.psum(mixed_part, 'expert')  26.3 us
    dot_general x1, matrix products, local(): jnp.einsum('enh,ehd->ned', hidden, down_weight, preferred_element_type=jn...  8.03 us
  transfers between devices with their start and end apart: 3, of which 3 were waited for; matrix products, arithmetic and copies ran while one was open for 0% of the time, Pallas kernels for 0%

commit v1 on v0

--- a/solution.py
+++ b/solution.py
@@ -5,6 +5,11 @@
 
 EXPERTS = 8
 CAP = 48
+
+
+def gather_over(array, name, dim):
+    repeated = jnp.stack([array] * lax.axis_size(name))
+    return jnp.concatenate(lax.all_to_all(repeated, name, 0, 0), axis=dim)
 
 
 def local(tokens, expert_ids, route_weights, gate_weight, up_weight, down_weight):
@@ -27,7 +32,7 @@
     picked = jnp.einsum("tec,tf->ecf", dispatch, tokens, preferred_element_type=jnp.float32).astype(
         jnp.bfloat16
     )
-    shard_rows = lax.all_gather(picked, "dp", axis=1, tiled=True)
+    shard_rows = gather_over(picked, "dp", 1)
     gate_part = jnp.einsum(
         "enf,efh->enh", shard_rows, gate_weight, preferred_element_type=jnp.float32
     )

time: 316 us -> 384 us (1.22)
  blocking collectives: 26.3 us -> 141 us
  waiting for transfers between devices: 249 us -> 203 us
    all_to_all x0 -> x1, blocking collectives: none -> 114 us  [gather_over(): return jnp.concatenate(lax.all_to_all(repeated, name, 0, 0), axis=dim)]
    all_gather x1 -> x0, waiting for transfers between devices: 45.8 us -> none  [local(): shard_rows = lax.all_gather(picked, 'dp', axis=1, tiled=True)]
  transfers between devices with their start and end apart: 3 -> 2, of which waited for: 3 -> 2; matrix products, arithmetic and copies ran while one was open for 0% -> 0% of each run, Pallas kernels for 0% -> 0%
where the time goes in v1:
time: 384 us
  waiting for transfers between devices  203 us (53%)
  blocking collectives  141 us (37%)
  matrix products  17.2 us (4%)
  between operations  13.5 us (4%)
  other arithmetic  4.9 us (1%)
  local copies, waits for them, and re-layouts  4.7 us (1%)
    psum x1, waiting for transfers between devices, local(): summed = lax.psum(partial_value, 'blk')  130 us
    all_to_all x1, blocking collectives, gather_over(): return jnp.concatenate(lax.all_to_all(repeated, name, 0, 0), axis=dim)  114 us
    reduce_scatter x1, waiting for transfers between devices, local(): lax.psum_scatter(jnp.einsum('enh,ehd->ned', hidden, down_weight, preferre...  73 us
    psum x1, blocking collectives, local(): mixed = lax.psum(mixed_part, 'expert')  26.4 us
    dot_general x1, matrix products, local(): jnp.einsum('enh,ehd->ned', hidden, down_weight, preferred_element_type=jn...  8.04 us
  transfers between devices with their start and end apart: 2, of which 2 were waited for; matrix products, arithmetic and copies ran while one was open for 0% of the time, Pallas kernels for 0%

profile of v1, /device:TPU:2, one launch (start us, length us, event | category | flops | bytes accessed | tf_op | source)
XLA Modules:
  0.0 383.7 jit_solution(17837398546231954809)
XLA Ops:
  6.5 0.9 copy.18
  7.5 0.1 eq.65
  7.6 0.1 reshape.78
  7.8 0.6 reduce-window.6
  8.4 0.2 slice_reduce_fusion
  8.6 0.1 fusion.7
  8.7 0.1 eq.69
  8.9 0.1 copy.20
  9.0 0.7 broadcast_subtract_fusion
  9.7 1.2 convolution_convert_fusion
  10.9 0.5 stack.8
  11.4 114.3 %all_to_all.5 = bf16[16,2,48,1536]{3,2,1,0:T(8,128)(2,1)S(1)} all-to-all(bf16[16,2,48,1536]{3,2,1,0:T(8,128)(2,1)S(1)} %stack.8), channel_id=1, replica_groups=mesh['dp'=16,'expert'=4,'blk'=4] {'dp'}, dimensions={0} | all-to-all | bytes 9437184 | tf_op jit(solution)/shard_map/all_to_all | solution.py:12
  125.7 0.4 copy.21
  126.1 1.5 copy-done.2
  127.6 2.6 convolution_bitcast_fusion.2
  130.2 2.6 convolution_bitcast_fusion.3
  132.8 3.4 pad_maximum_fusion
  136.3 0.0 reduce-scatter.2.cloned.1.call-start
  136.3 129.6 %all-reduce.3.cloned.1.call-done = f32[2,2,768,512]{3,2,1,0:T(8,128)} async-done(((f32[2,2,768,512]{3,2,1,0:T(8,128)}), f32[2,2,768,512]{3,2,1,0:T(8,128)}) %all-reduce.3.cloned.1.call-update) | async-done | bytes 6291472 | tf_op jit(solution)/shard_map/psum | solution.py:41
  266.0 8.0 %convolution_bitcast_fusion = f32[768,2,1536]{2,0,1:T(8,128)} fusion(bf16[2,512,1536]{2,1,0:T(8,128)(2,1)S(1)} %copy-done, f32[2,2,768,512]{3,2,1,0:T(8,128)} %all-reduce.3.cloned.1.call-done), kind=kOutput, calls=%fused_computation.1 | convolution fusion | flops 2420637696 | bytes 18874368 | tf_op jit(solution)/shard_map/enh,ehd->ned/dot_general | solution.py:44
  274.0 0.7 copy-done.1
  274.7 73.0 %reduce-scatter.2.cloned.1.call-done = f32[48,2,1536]{2,0,1:T(8,128)} async-done(((f32[768,2,1536]{2,0,1:T(8,128)}), f32[48,2,1536]{2,0,1:T(8,128)}) %reduce-scatter.2.cloned.1.call-update) | async-done | bytes 589840 | tf_op jit(solution)/shard_map/reduce_scatter | solution.py:43
  347.7 2.8 convolution_bitcast_fusion.1
  350.4 26.4 %all-reduce.4 = bf16[128,1536]{1,0:T(8,128)(2,1)} all-reduce(f32[128,1536]{1,0:T(8,128)} %convolution_bitcast_fusion.1), channel_id=1, replica_groups=mesh['dp'=16,'expert'=4,'blk'=4] {'expert'}, use_global_device_ids=true, to_apply=%region_7.8 | all-reduce | flops 196608 | bytes 1179648 | tf_op jit(solution)/shard_map/psum | solution.py:50
  (16 shorter events, 0.2 us)
Async XLA Ops:
  6.5 259.4 %copy-start = (bf16[2,512,1536]{2,1,0:T(8,128)(2,1)S(1)}, bf16[2,512,1536]{2,1,0:T(8,128)(2,1)}, u32[]{:S(2)}) copy-start(bf16[2,512,1536]{2,1,0:T(8,128)(2,1)} %param.11) | copy-start | bytes 9437188
  6.5 259.4 %all-reduce.3.cloned.1.call-start = ((), (), s32[]{:S(2)}) async-start(), calls=%async_computation.2 | async-start | bytes 12582912 | tf_op jit(solution)/shard_map/psum | solution.py:41
  125.7 1.9 copy-start.2
  127.6 2.6 copy-start.3
  136.3 211.4 %reduce-scatter.2.cloned.1.call-start = ((), (), s32[]{:S(2)}) async-start(), calls=%async_computation.3 | async-start | bytes 10027008 | tf_op jit(solution)/shard_map/reduce_scatter | solution.py:43
  274.0 0.7 copy-start.1
Sparse Core Ops, SparseCore 0:
  136.4 129.5 all-reduce.2
  274.1 73.4 reduce-scatter.1
